TPU v7x, 128 devices: a whole 4x4x4 slice. The times are simulated.
128 devices in a mesh: expert: 2 (over y_hi), fsdp: 64 (over x, y_lo, z, core).
Axes of the slice: x: 4, y: 4 (y_hi: 2, y_lo: 2; y = y_hi * 2 + y_lo), z: 4, core: 2. Of those that a mesh axis runs over, the one named last changes fastest.
Arguments:
- query_rows: bfloat16 [32768, 2560], P(('expert', 'fsdp')), may hold values from -16 to 16
- key_rows: bfloat16 [32768, 2560], P(('expert', 'fsdp')), may hold values from -16 to 16
- value_rows: bfloat16 [32768, 2560], P(('expert', 'fsdp')), may hold values from -6 to 6
- timestep: int32 [32], replicated, may hold values from 0 to 999, as said below
- time_weight: bfloat16 [2, 256, 5120], P('expert', None, 'fsdp'), may hold values from -0.375 to 0.375
- gate_weight: bfloat16 [2, 5120, 2560], P('expert', None, 'fsdp'), may hold values from -0.078125 to 0.078125
- cotangent: bfloat16 [32768, 2560], P(('expert', 'fsdp')), may hold values from -6 to 6
Outputs:
- gated: bfloat16 [32768, 2560], P(('expert', 'fsdp'))
- query_grad: bfloat16 [32768, 2560], P(('expert', 'fsdp'))
- key_grad: bfloat16 [32768, 2560], P(('expert', 'fsdp'))
- value_grad: bfloat16 [32768, 2560], P(('expert', 'fsdp'))
- time_grad: float32 [2, 256, 5120], P('expert', None, 'fsdp')
- gate_grad: float32 [2, 5120, 2560], P('expert', None, 'fsdp')
Inputs may be any that keep to these rules, and one draw needn't show every extreme that they name: Exactly half of the clips have a timestep of 875 or more.
All inputs are finite; a program needn't handle non-finite values.
Results may differ from a plain program's by a relative error of at most 0.03.
Values may be sent and summed in bfloat16 or wider, within the bound.
A program may use at most 192 MiB of HBM per device.

v0:
```python
import math

import jax
import jax.numpy as jnp
from jax import lax
from jax.sharding import PartitionSpec as P

FREQ = 256
HEAD = 128
HEADS = 20
BOUNDARY = 875
SPAN = 4


def swapped(block, axis, stride):
    count = lax.axis_size(axis)
    route = []
    for low in range(count):
        high = low | 1 << stride
        if high != low and high < count:
            route += [(low, high), (high, low)]
    return lax.ppermute(block, axis, route)


def from_behind(value, axis, steps):
    count = lax.axis_size(axis)
    pairs = [(source, (source + steps) % count) for source in range(count)]
    return lax.ppermute(value, axis, pairs)


def sinusoid(timestep):
    half_freq = FREQ // 2
    indices = jnp.arange(half_freq, dtype=jnp.float32)
    frequency = jnp.exp(-math.log(10000.0) * indices / half_freq)
    angles = timestep.astype(jnp.float32)[:, None] * frequency[None, :]
    return jnp.concatenate([jnp.cos(angles), jnp.sin(angles)], axis=1)


def heads_view(rows):
    return rows.reshape(rows.shape[0], HEADS, HEAD)


def per_device(query_rows, key_rows, value_rows, timestep, time_weight, gate_weight, cotangent):
    highest = lax.Precision.HIGHEST
    stride = lax.axis_size("fsdp") // SPAN
    own_half = lax.axis_index("expert")
    position = lax.axis_index("fsdp")
    row_count = query_rows.shape[0]
    scaling = HEAD ** (-0.5)
    expert_of = (timestep >= BOUNDARY).astype(jnp.int32)
    own_clips = (expert_of == own_half)[:, None]
    sinusoid_rows = sinusoid(timestep)
    emb_cols = jnp.dot(sinusoid_rows, time_weight[0].astype(jnp.float32), precision=highest).astype(
        jnp.bfloat16
    )
    embedding = lax.all_gather(emb_cols, "fsdp", axis=1, tiled=True)
    activated = jax.nn.silu(embedding.astype(jnp.float32)).astype(jnp.bfloat16)
    gate_cols = jnp.dot(activated, gate_weight[0], preferred_element_type=jnp.float32).astype(
        jnp.bfloat16
    )
    partner = swapped(gate_cols, "expert", 0)
    chosen = jnp.where(own_clips, gate_cols, partner)
    gate_table = lax.all_gather(chosen, "fsdp", axis=1, tiled=True)
    clip_index = own_half * stride + position % stride
    gate_row = lax.dynamic_index_in_dim(gate_table, clip_index, 0, keepdims=False).astype(
        jnp.float32
    )
    stacked = jnp.stack([key_rows, value_rows])
    received = [from_behind(stacked, "fsdp", step * stride) for step in range(1, SPAN)]
    gathered = jnp.concatenate([stacked] + received, axis=1)
    keys_all = heads_view(gathered[0])
    values_all = heads_view(gathered[1])
    queries = heads_view(query_rows)
    scores = (
        jnp.einsum("qhd,khd->hqk", queries, keys_all, preferred_element_type=jnp.float32) * scaling
    )
    top = jnp.max(scores, axis=2, keepdims=True)
    expo = jnp.exp(scores - top)
    total = jnp.sum(expo, axis=2, keepdims=True)
    probability = expo / total
    prob_half = probability.astype(jnp.bfloat16)
    attended = jnp.einsum("hqk,khd->qhd", prob_half, values_all, preferred_element_type=jnp.float32)
    attended = attended.reshape(row_count, -1).astype(jnp.bfloat16)
    gated = (gate_row[None, :] * attended.astype(jnp.float32)).astype(jnp.bfloat16)
    d_attended = (cotangent.astype(jnp.float32) * gate_row[None, :]).astype(jnp.bfloat16)
    gate_local = jnp.sum(cotangent.astype(jnp.float32) * attended.astype(jnp.float32), axis=0)
    d_heads = heads_view(d_attended)
    delta = jnp.sum(
        heads_view(d_attended.astype(jnp.float32) * attended.astype(jnp.float32)), axis=2
    ).T
    d_prob = jnp.einsum("qhd,khd->hqk", d_heads, values_all, preferred_element_type=jnp.float32)
    d_scores = (probability * (d_prob - delta[:, :, None]) * scaling).astype(jnp.bfloat16)
    query_grad = jnp.einsum("hqk,khd->qhd", d_scores, keys_all, preferred_element_type=jnp.float32)
    query_grad = query_grad.reshape(row_count, -1).astype(jnp.bfloat16)
    key_part = jnp.einsum("hqk,qhd->khd", d_scores, queries, preferred_element_type=jnp.float32)
    value_part = jnp.einsum("hqk,qhd->khd", prob_half, d_heads, preferred_element_type=jnp.float32)
    partial_grads = jnp.stack(
        [key_part.reshape(SPAN, row_count, -1), value_part.reshape(SPAN, row_count, -1)], axis=1
    )
    summed = partial_grads[0]
    for step in range(1, SPAN):
        summed = summed + from_behind(partial_grads[step], "fsdp", -step * stride)
    key_grad = summed[0].astype(jnp.bfloat16)
    value_grad = summed[1].astype(jnp.bfloat16)
    clip_numbers = jnp.arange(gate_table.shape[0])
    placed = jnp.where((clip_numbers == clip_index)[:, None], gate_local[None, :], 0.0)
    half_sums = lax.psum_scatter(placed, "fsdp", scatter_dimension=1, tiled=True)
    both_halves = lax.psum(half_sums, "expert")
    d_gate = jnp.where(own_clips, both_halves, 0.0)
    gate_grad = jnp.dot(activated.astype(jnp.float32).T, d_gate, precision=highest)[None]
    d_act_part = jnp.dot(d_gate, gate_weight[0].astype(jnp.float32).T, precision=highest)
    d_act = lax.psum_scatter(d_act_part, "fsdp", scatter_dimension=1, tiled=True)
    emb_f = emb_cols.astype(jnp.float32)
    sigmoid_e = jax.nn.sigmoid(emb_f)
    d_emb = d_act * sigmoid_e * (1.0 + emb_f * (1.0 - sigmoid_e))
    time_grad = jnp.dot(sinusoid_rows.T, d_emb, precision=highest)[None]
    return (gated, query_grad, key_grad, value_grad, time_grad, gate_grad)


def solution(mesh):
    return jax.shard_map(
        per_device,
        mesh=mesh,
        in_specs=(
            P(("expert", "fsdp"), None),
            P(("expert", "fsdp"), None),
            P(("expert", "fsdp"), None),
            P(),
            P("expert", None, "fsdp"),
            P("expert", None, "fsdp"),
            P(("expert", "fsdp"), None),
        ),
        out_specs=(
            P(("expert", "fsdp"), None),
            P(("expert", "fsdp"), None),
            P(("expert", "fsdp"), None),
            P(("expert", "fsdp"), None),
            P("expert", None, "fsdp"),
            P("expert", None, "fsdp"),
        ),
        check_vma=False,
    )
```

profile of v0, /device:TPU:24, one launch (start us, length us, event | category | flops | bytes accessed | tf_op | source)
XLA Modules:
  0.0 1453.8 jit_solution(10660046546156422176)
XLA Ops:
  12.3 2.8 collective-permute-start.3
  18.1 178.3 %all-gather = bf16[64,80,32]{1,2,0:T(8,128)(2,1)S(1)} all-gather(bf16[1,80,32]{1,2,0:T(8,128)(2,1)S(1)} %bitcast.135), channel_id=1, replica_groups=mesh['expert'=2,'fsdp'=64] {'fsdp'}, dimensions={0}, use_global_device_ids=true | all-gather | bytes 332800 | tf_op jit(solution)/shard_map/all_gather | solution.py:56
  197.6 2.7 reshape.55
  202.9 2.4 copy.60
  205.4 2.4 copy.56
  207.9 80.1 %all-gather.1 = bf16[64,40,32]{1,2,0:T(8,128)(2,1)S(1)} all-gather(bf16[1,40,32]{1,2,0:T(8,128)(2,1)S(1)} %select_bitcast_fusion), channel_id=1, replica_groups=mesh['expert'=2,'fsdp'=64] {'fsdp'}, dimensions={0}, use_global_device_ids=true | all-gather | bytes 166400 | tf_op jit(solution)/shard_map/all_gather | solution.py:63
  290.4 9.1 pad_maximum_fusion
  299.5 9.4 fusion.51
  308.9 12.8 fusion.52
  321.8 9.5 fusion.7
  331.3 4.3 bitcast_multiply_fusion
  335.6 8.8 convolution_bitcast_fusion.2
  346.3 14.8 %multiply_convert_fusion = bf16[20,256,1024]{1,2,0:T(8,128)(2,1)} fusion(f32[20,256]{1,0:T(8,128)S(1)} %bitcast.137, bf16[256,20,128]{0,2,1:T(8,128)(2,1)} %bitcast.132, bf16[1024,20,128]{0,2,1:T(8,128)(2,1)} %bitcast.123, f32[20,256,1024]{1,2,0:T(8,128)} %get-tuple-element.39, f32[20,256]{1,0:T(8,128)S(1)} %get-tuple-element.38), kind=kOutput, calls=%fused_computation.5 | convolution fusion | flops 1368391680 | bytes 38051840 | tf_op jit(solution)/shard_map/qhd,khd->hqk/dot_general | solution.py:91
  361.1 10.8 convolution_bitcast_fusion.3
  371.9 11.4 copy.66
  383.3 13.0 stack_reshape.6
  396.3 10.3 constant_dynamic-update-slice_fusion.1
  406.6 13.0 stack_reshape.7
  419.7 10.4 constant_dynamic-update-slice_fusion
  430.0 38.5 %fusion.50 = (f32[1,2,256,2560]{2,0,3,1:T(1,128)}, f32[1,2,256,2560]{2,0,3,1:T(1,128)}, f32[1,2,256,2560]{2,0,3,1:T(1,128)}, f32[1,2,256,2560]{2,0,3,1:T(1,128)}) fusion(f32[4,2,256,2560]{2,0,3,1:T(4,128)} %constant_dynamic-update-slice_fusion), kind=kLoop, calls=%fused_computation.83 | loop fusion | bytes 41943040 | tf_op jit(solution)/shard_map/slice | solution.py:100
  468.5 5.7 copy.106
  474.2 2.7 copy.104
  476.9 2.0 collective-permute-start.5
  479.0 2.6 copy.105
  485.0 656.8 %all-reduce.3.cloned.1.call-done = f32[32,2560]{1,0:T(8,128)} async-done(((f32[32,2560]{1,0:T(8,128)}), f32[32,2560]{1,0:T(8,128)}) %all-reduce.3.cloned.1.call-update) | async-done | bytes 327696
  1142.6 9.6 psum.7
  1152.2 3.1 convolution_bitcast_fusion
  1157.1 7.1 convolution_convert_fusion
  1167.4 263.0 %reduce-scatter.5.cloned.1.call-done = f32[80,32]{1,0:T(8,128)} async-done(((f32[5120,32]{1,0:T(8,128)}), f32[80,32]{1,0:T(8,128)}) %reduce-scatter.5.cloned.1.call-update) | async-done | bytes 10256
  1432.2 8.2 fusion.11
  1442.1 2.4 copy.73
  1444.5 2.4 copy.74
  (84 shorter events, 28.3 us)
Async XLA Ops:
  7.2 193.1 %copy-start = (bf16[1,5120,40]{1,2,0:T(8,128)(2,1)S(1)}, bf16[1,5120,40]{1,2,0:T(8,128)(2,1)}, u32[]{:S(2)}) copy-start(bf16[1,5120,40]{1,2,0:T(8,128)(2,1)} %param.12) | copy-start | bytes 1228804
  7.2 9.6 copy-start.17
  7.2 9.7 copy-start.14
  7.2 1134.6 %all-reduce.3.cloned.1.call-start = ((), (), s32[]{:S(2)}) async-start(), calls=%async_computation.2 | async-start | bytes 655360
  12.3 278.1 %collective-permute-start.3 = (bf16[2,256,2560]{1,2,0:T(8,128)(2,1)}, bf16[2,256,2560]{1,2,0:T(8,128)(2,1)}, u32[]{:S(2)}, u32[]{:S(2)}) collective-permute-start(bf16[2,256,2560]{1,2,0:T(8,128)(2,1)} %pad_maximum_fusion.1), channel_id=1, source_target_pairs={{0,48},{1,49},{2,50},{3,51},{4,52},{5,53},{6,54},{7,55},{8,56},{9,... | collective-permute-start | bytes 7864328 | tf_op jit(solution)/shard_map/ppermute | solution.py:28
  15.1 275.4 %collective-permute-start.2 = (bf16[2,256,2560]{1,2,0:T(8,128)(2,1)}, bf16[2,256,2560]{1,2,0:T(8,128)(2,1)}, u32[]{:S(2)}, u32[]{:S(2)}) collective-permute-start(bf16[2,256,2560]{1,2,0:T(8,128)(2,1)} %pad_maximum_fusion.1), channel_id=1, source_target_pairs={{0,32},{1,33},{2,34},{3,35},{4,36},{5,37},{6,38},{7,39},{8,40},{9,... | collective-permute-start | bytes 7864328 | tf_op jit(solution)/shard_map/ppermute | solution.py:28
  15.9 274.6 %collective-permute-start.1 = (bf16[2,256,2560]{1,2,0:T(8,128)(2,1)}, bf16[2,256,2560]{1,2,0:T(8,128)(2,1)}, u32[]{:S(2)}, u32[]{:S(2)}) collective-permute-start(bf16[2,256,2560]{1,2,0:T(8,128)(2,1)} %pad_maximum_fusion.1), channel_id=1, source_target_pairs={{0,16},{1,17},{2,18},{3,19},{4,20},{5,21},{6,22},{7,23},{8,24},{9,... | collective-permute-start | bytes 7864328 | tf_op jit(solution)/shard_map/ppermute | solution.py:28
  16.9 0.6 copy-start.8
  16.9 0.6 copy-start.10
  17.5 0.6 copy-start.12
  201.6 6.2 collective-permute-start
  202.9 4.9 copy-start.15
  299.5 9.4 copy-start.5
  321.8 9.5 copy-start.2
  321.8 9.5 copy-start.4
  346.3 14.8 %copy-start.6 = (bf16[256,2560]{0,1:T(8,128)(2,1)S(1)}, bf16[256,2560]{0,1:T(8,128)(2,1)}, u32[]{:S(2)}) copy-start(bf16[256,2560]{0,1:T(8,128)(2,1)} %copy.56) | copy-start | bytes 3932164
  468.5 5.7 copy-start.1
  468.5 10.4 slice-start
  474.2 4.8 slice-start.1
  474.2 958.0 %collective-permute-start.6 = (f32[2,256,2560]{1,2,0:T(8,128)}, f32[2,256,2560]{1,2,0:T(8,128)}, u32[]{:S(2)}, u32[]{:S(2)}) collective-permute-start(f32[2,256,2560]{1,2,0:T(8,128)} %bitcast.118), channel_id=1, source_target_pairs={{0,16},{1,17},{2,18},{3,19},{4,20},{5,21},{6,22},{7,23},{8,24},{9,... | collective-permute-start | bytes 15728648 | tf_op jit(solution)/shard_map/ppermute | solution.py:28
  476.9 955.3 %collective-permute-start.5 = (f32[2,256,2560]{1,2,0:T(8,128)}, f32[2,256,2560]{1,2,0:T(8,128)}, u32[]{:S(2)}, u32[]{:S(2)}) collective-permute-start(f32[2,256,2560]{1,2,0:T(8,128)} %bitcast.116), channel_id=1, source_target_pairs={{0,32},{1,33},{2,34},{3,35},{4,36},{5,37},{6,38},{7,39},{8,40},{9,... | collective-permute-start | bytes 15728648 | tf_op jit(solution)/shard_map/ppermute | solution.py:28
  479.0 4.7 copy-start.18
  479.0 673.2 %copy-start.16 = (pred[32]{0:T(512)(128)(4,1)S(1)}, pred[32]{0:T(512)(128)(4,1)}, u32[]{:S(2)}) copy-start(pred[32]{0:T(512)(128)(4,1)} %copy-done.15) | copy-start | bytes 100
  481.6 673.7 %copy-start.3 = (bf16[256,2560]{0,1:T(8,128)(2,1)S(1)}, bf16[256,2560]{0,1:T(8,128)(2,1)}, u32[]{:S(2)}) copy-start(bf16[256,2560]{0,1:T(8,128)(2,1)} %get-tuple-element.35) | copy-start | bytes 3932164
  481.6 950.6 %collective-permute-start.4 = (f32[2,256,2560]{1,2,0:T(8,128)}, f32[2,256,2560]{1,2,0:T(8,128)}, u32[]{:S(2)}, u32[]{:S(2)}) collective-permute-start(f32[2,256,2560]{1,2,0:T(8,128)} %bitcast.117), channel_id=1, source_target_pairs={{0,48},{1,49},{2,50},{3,51},{4,52},{5,53},{6,54},{7,55},{8,56},{9,... | collective-permute-start | bytes 15728648 | tf_op jit(solution)/shard_map/ppermute | solution.py:28
  483.7 946.8 %reduce-scatter.5.cloned.1.call-start = ((), (), s32[]{:S(2)}) async-start(), calls=%async_computation.1 | async-start | bytes 2662400
  1157.1 8.8 copy-start.7
  1164.3 267.0 %copy-start.9 = (f32[32,128]{1,0:T(8,128)S(1)}, f32[32,128]{1,0:T(8,128)}, u32[]{:S(2)}) copy-start(f32[32,128]{1,0:T(8,128)} %copy-done.8) | copy-start | bytes 49156
  1164.3 267.0 %copy-start.11 = (f32[32,128]{1,0:T(8,128)S(1)}, f32[32,128]{1,0:T(8,128)}, u32[]{:S(2)}) copy-start(f32[32,128]{1,0:T(8,128)} %copy-done.10) | copy-start | bytes 49156
  1164.3 267.0 %copy-start.13 = (bf16[32,80]{1,0:T(8,128)(2,1)S(1)}, bf16[32,80]{1,0:T(8,128)(2,1)}, u32[]{:S(2)}) copy-start(bf16[32,80]{1,0:T(8,128)(2,1)} %copy-done.12) | copy-start | bytes 15364
Sparse Core Ops, SparseCore 0:
  483.8 657.9 all-reduce.2
  1155.4 274.9 reduce-scatter.4
where the time goes:
time: 1480 us; the launch traced here: 1450 us
  waiting for transfers between devices  920 us (62%)
  blocking collectives  268 us (18%)
  local copies, waits for them, and re-layouts  144 us (10%)
  matrix products  65.7 us (4%)
  other arithmetic  32.4 us (2%)
  between operations  15 us (1%)
    unnamed x4, waiting for transfers between devices  920 us
    all_gather x1, blocking collectives, per_device(): embedding = lax.all_gather(emb_cols, 'fsdp', axis=1, tiled=True)  178 us
    all_gather x1, blocking collectives, per_device(): gate_table = lax.all_gather(chosen, 'fsdp', axis=1, tiled=True)  80.1 us
    unnamed x58, local copies, waits for them, and re-layouts  42.3 us
    slice x1, local copies, waits for them, and re-layouts, per_device(): summed = partial_grads[0]  38.5 us
    another operation x3, local copies, waits for them, and re-layouts, per_device(): jnp.stack([key_part.reshape(SPAN, row_count, -1), value_part.reshape(SPAN...  36.4 us
  transfers between devices with their start and end apart: 9, of which 2 were waited for; matrix products, arithmetic and copies ran while one was open for 3% of the time, Pallas kernels for 0%

commit v1 on v0

v1 whole, which is shorter than its diff:
```python
import math

import jax
import jax.numpy as jnp
from jax import lax
from jax.experimental import pallas as pl
from jax.experimental.pallas import tpu as pltpu
from jax.sharding import PartitionSpec as P

FREQ = 256
HEAD = 128
BOUNDARY = 875
SPAN = 4
ROWS = 256
OWN = 5
CLIP = SPAN * ROWS
NCLIP = 32
EMB = 80
COLS = 40
D = 5120
DH = 2560
GROUP = 8 * EMB
QB = 256
MESH = pl.DeviceIdType.MESH
F32 = jnp.float32
BF16 = jnp.bfloat16
NT = (((1,), (1,)), ((), ()))
NN = (((1,), (0,)), ((), ()))


def dot(a, b, dims=NN):
    return lax.dot_general(a, b, dims, preferred_element_type=F32)


def split3(value):
    high = value.astype(BF16)
    rest = value - high.astype(F32)
    middle = rest.astype(BF16)
    return high, middle, (rest - middle.astype(F32)).astype(BF16)


def exact_dot(a, b, dims=NN):
    parts = split3(a)
    return dot(parts[0], b, dims) + (dot(parts[1], b, dims) + dot(parts[2], b, dims))


def kernel(
    ts, q_in, k_in, v_in, c_in, tw, gw,
    gated, query_grad, key_grad, value_grad, time_grad, gate_grad,
    buf, ost, emb, own_emb, act, sins, cols, cols_in, table, gate_rows,
    dg_own, dg_all, parts, sum_core, sum_z, sum_y, in_core, in_z, in_y, in_x,
    key_t, value_t, key_acc, value_acc,
    send_sems, recv_sems, in_send, in_recv, out_send, out_recv,
):
    half = lax.axis_index("expert")
    fsdp = lax.axis_index("fsdp")
    core = lax.rem(fsdp, 2)
    z = lax.rem(lax.div(fsdp, 2), 4)
    y = lax.rem(lax.div(fsdp, 8), 2)
    x = lax.div(fsdp, 16)
    plane = lax.rem(fsdp, 16)

    def place(x_, y_, z_, core_):
        return {"fsdp": x_ * 16 + y_ * 8 + z_ * 2 + core_}

    x_at = [lax.rem(x + d, 4) for d in (1, 2, 3)]
    z_at = [lax.rem(z + d, 4) for d in (1, 2, 3)]
    x_peers = [place(p, y, z, core) for p in x_at]
    z_peers = [place(x, y, p, core) for p in z_at]
    y_peer = place(x, 1 - y, z, core)
    core_peer = place(x, y, z, 1 - core)
    half_peer = {"expert": 1 - half}
    peers = x_peers + z_peers + [y_peer, core_peer, half_peer]

    barrier = pltpu.get_barrier_semaphore()
    for peer in peers:
        pl.semaphore_signal(barrier, inc=1, device_id=peer, device_id_type=MESH)

    used = [0]

    def begin(moves):
        copies = []
        for source, target, peer in moves:
            slot = used[0]
            used[0] += 1
            copy = pltpu.make_async_remote_copy(
                src_ref=source,
                dst_ref=target,
                send_sem=send_sems.at[slot],
                recv_sem=recv_sems.at[slot],
                device_id=peer,
                device_id_type=MESH,
            )
            copy.start()
            copies.append(copy)
        return copies

    def exchange(moves):
        for copy in begin(moves):
            copy.wait()

    row = lax.broadcasted_iota(jnp.int32, (NCLIP, HEAD), 0)
    lane = lax.broadcasted_iota(jnp.int32, (8, HEAD), 1)
    step_rows = jnp.zeros((NCLIP, HEAD), jnp.int32)
    step_lanes = jnp.zeros((8, HEAD), jnp.int32)
    for clip in range(NCLIP):
        step_rows = jnp.where(row == clip, ts[clip], step_rows)
        step_lanes = jnp.where(lane == clip, ts[clip], step_lanes)
    own_rows = (step_rows >= BOUNDARY).astype(jnp.int32) == half
    own_lanes = (step_lanes >= BOUNDARY).astype(jnp.int32) == half

    index = lax.broadcasted_iota(jnp.int32, (NCLIP, HEAD), 1).astype(F32)
    frequency = jnp.exp(-math.log(10000.0) * index / (FREQ // 2))
    angles = step_rows.astype(F32) * frequency
    sins[:, 0:HEAD] = jnp.cos(angles)
    sins[:, HEAD:FREQ] = jnp.sin(angles)
    emb_cols = exact_dot(sins[...], tw[...], NT)
    own_emb[...] = jnp.zeros(own_emb.shape, F32)
    own_emb[:, 0:EMB] = emb_cols
    emb[x, y, z, core] = own_emb[...].astype(BF16)

    pl.semaphore_wait(barrier, len(peers))

    first = begin([(emb.at[x, y, z, core], emb.at[x, y, z, core], peer) for peer in x_peers])
    sources = (q_in, k_in, v_in, c_in)

    def send_head(head, carry):
        for which, source in enumerate(sources):
            for to, peer in zip(x_at, x_peers):
                pltpu.make_async_remote_copy(
                    src_ref=source.at[:, pl.ds(pl.multiple_of((to * OWN + head) * HEAD, HEAD), HEAD)],
                    dst_ref=buf.at[head, which, pl.ds(pl.multiple_of(x * ROWS, ROWS), ROWS), :],
                    send_sem=in_send,
                    recv_sem=in_recv.at[head],
                    device_id=peer,
                    device_id_type=MESH,
                ).start()
            pltpu.make_async_copy(
                source.at[:, pl.ds(pl.multiple_of((x * OWN + head) * HEAD, HEAD), HEAD)],
                buf.at[head, which, pl.ds(pl.multiple_of(x * ROWS, ROWS), ROWS), :],
                in_recv.at[head],
            ).start()
        return carry

    lax.fori_loop(0, OWN, send_head, 0)

    for copy in first:
        copy.wait()
    exchange([(emb.at[:, y, z, core], emb.at[:, y, z, core], y_peer)])
    exchange([(emb.at[:, :, z, core], emb.at[:, :, z, core], peer) for peer in z_peers])
    exchange([(emb.at[:, :, :, core], emb.at[:, :, :, core], core_peer)])

    def activate(group, carry):
        x_, y_ = lax.div(group, 2), lax.rem(group, 2)
        blocks = [emb[x_, y_, j // 2, j % 2].astype(F32)[:, 0:EMB] for j in range(8)]
        value = jnp.concatenate(blocks, axis=1)
        value = value / (1.0 + jnp.exp(-value))
        act[:, pl.ds(pl.multiple_of(group * GROUP, GROUP), GROUP)] = value.astype(BF16)
        return carry

    lax.fori_loop(0, 8, activate, 0)
    gate_cols = dot(gw[...], act[...], NT).astype(BF16).astype(F32)
    cols[...] = jnp.zeros(cols.shape, F32)
    cols[:, 0:NCLIP] = gate_cols
    exchange([(cols, cols_in, half_peer)])
    table[y, z, core] = jnp.where(own_lanes[0:1], cols[...], cols_in[...])
    exchange([(table.at[y, z, core], table.at[y, z, core], peer) for peer in z_peers])
    exchange([(table.at[y, :, core], table.at[y, :, core], y_peer)])
    exchange([(table.at[:, :, core], table.at[:, :, core], core_peer)])
    whole = table[...].reshape(OWN * HEAD, HEAD)
    for head in range(OWN):
        gate_rows[head] = whole[head * HEAD : (head + 1) * HEAD].T
    clip_index = half * 16 + plane

    scaling = HEAD ** (-0.5)
    dg_own[...] = jnp.zeros(dg_own.shape, F32)

    def attend(head):
        pltpu.make_async_copy(buf.at[head], buf.at[head], in_recv.at[head]).wait()
        keys = buf[head, 1]
        values = buf[head, 2]
        key_t[...] = keys.T
        value_t[...] = values.T
        gate = gate_rows[head, pl.ds(clip_index, 1), :]
        key_acc[...] = jnp.zeros(key_acc.shape, F32)
        value_acc[...] = jnp.zeros(value_acc.shape, F32)

        def block(step, d_gate):
            rows = pl.ds(pl.multiple_of(step * QB, QB), QB)
            queries = buf[head, 0, rows, :]
            scores = dot(buf[head, 1], queries, NT)
            top = jnp.max(scores, axis=0, keepdims=True)
            expo = jnp.exp2((scores - top) * (scaling * math.log2(math.e)))
            probability = expo * (1.0 / jnp.sum(expo, axis=0, keepdims=True))
            prob_half = probability.astype(BF16)
            attended = dot(value_t[...], prob_half).T.astype(BF16).astype(F32)
            cotangent = buf[head, 3, rows, :].astype(F32)
            ost[head, 0, rows, :] = (gate * attended).astype(BF16)
            d_attended = (cotangent * gate).astype(BF16)
            delta = jnp.sum((d_attended.astype(F32) * attended).T, axis=0, keepdims=True)
            d_prob = dot(buf[head, 2], d_attended, NT)
            d_scores = (probability * (d_prob - delta)).astype(BF16)
            key_acc[...] += dot(d_scores, queries)
            value_acc[...] += dot(prob_half, d_attended)
            d_query = dot(key_t[...], d_scores).T * scaling
            ost[head, 1, rows, :] = d_query.astype(BF16)
            return d_gate + jnp.sum(cotangent * attended, axis=0, keepdims=True)

        d_gate = lax.fori_loop(0, CLIP // QB, block, jnp.zeros((1, HEAD), F32))
        ost[head, 2] = (key_acc[...] * scaling).astype(BF16)
        ost[head, 3] = value_acc[...].astype(BF16)
        dg_own[pl.ds(head, 1), :] = d_gate

    targets = (gated, query_grad, key_grad, value_grad)

    def send_out(head):
        at = pl.ds(pl.multiple_of((x * OWN + head) * HEAD, HEAD), HEAD)
        for which, target in enumerate(targets):
            for to, peer in zip(x_at, x_peers):
                pltpu.make_async_remote_copy(
                    src_ref=ost.at[head, which, pl.ds(pl.multiple_of(to * ROWS, ROWS), ROWS), :],
                    dst_ref=target.at[:, at],
                    send_sem=out_send,
                    recv_sem=out_recv.at[which],
                    device_id=peer,
                    device_id_type=MESH,
                ).start()
            pltpu.make_async_copy(
                ost.at[head, which, pl.ds(pl.multiple_of(x * ROWS, ROWS), ROWS), :],
                target.at[:, at],
                out_recv.at[which],
            ).start()

    def run_head(head, carry):
        attend(head)
        send_out(head)
        return carry

    lax.fori_loop(0, OWN - 1, run_head, 0)
    attend(OWN - 1)

    dg_all[half, y, z, core] = dg_own[...]
    exchange([(dg_all.at[half, y, z, core], dg_all.at[half, y, z, core], peer) for peer in z_peers])
    exchange([(dg_all.at[half, y, :, core], dg_all.at[half, y, :, core], y_peer)])
    exchange([(dg_all.at[half, :, :, core], dg_all.at[half, :, :, core], core_peer)])
    exchange([(dg_all.at[half], dg_all.at[half], half_peer)])
    everything = dg_all[...].reshape(NCLIP, 8, HEAD)
    d_rows = jnp.zeros((NCLIP, COLS), F32)
    d_cols = jnp.zeros((COLS, NCLIP), F32)
    pick_row = lax.broadcasted_iota(jnp.int32, (COLS, HEAD), 0) + plane * COLS
    pick_lane = lax.broadcasted_iota(jnp.int32, (COLS, HEAD), 1)
    for head in range(OWN):
        pick = (pick_row == pick_lane + head * HEAD).astype(F32).astype(BF16)
        for part in split3(everything[:, head, :]):
            d_rows = d_rows + dot(part, pick, NT)
            d_cols = d_cols + dot(pick, part, NT)
    d_rows = jnp.where(own_rows[:, 0:COLS], d_rows, 0.0)
    d_cols = jnp.where(own_lanes[0:1, 0:NCLIP], d_cols, 0.0)
    row_parts = split3(d_rows)
    col_parts = split3(d_cols)
    parts[...] = jnp.zeros(parts.shape, F32)

    def weight_group(group, carry):
        at = pl.ds(pl.multiple_of(group * GROUP, GROUP), GROUP)
        weights = gw[:, at]
        value = dot(row_parts[0], weights) + (dot(row_parts[1], weights) + dot(row_parts[2], weights))
        for j in range(8):
            parts[lax.div(group, 2), lax.rem(group, 2), j // 2, j % 2, :, 0:EMB] = value[
                :, j * EMB : (j + 1) * EMB
            ]
        return carry

    lax.fori_loop(0, 8, weight_group, 0)

    copies = begin([(parts.at[:, :, :, 1 - core], in_core, core_peer)])

    def grad_group(group, carry):
        at = pl.ds(pl.multiple_of(group * GROUP, GROUP), GROUP)
        a = act[:, at]
        gate_grad[:, at] = dot(col_parts[0], a) + (dot(col_parts[1], a) + dot(col_parts[2], a))
        return carry

    lax.fori_loop(0, 8, grad_group, 0)

    copies[0].wait()
    sum_core[...] = parts[:, :, :, core] + in_core[...]
    exchange([(sum_core.at[:, :, p], in_z.at[d], peer) for d, (p, peer) in enumerate(zip(z_at, z_peers))])
    sum_z[...] = sum_core[:, :, z] + ((in_z[0] + in_z[1]) + in_z[2])
    exchange([(sum_z.at[:, 1 - y], in_y, y_peer)])
    sum_y[...] = sum_z[:, y] + in_y[...]
    copies = begin([(sum_y.at[p], in_x.at[d], peer) for d, (p, peer) in enumerate(zip(x_at, x_peers))])
    send_out(OWN - 1)
    for copy in copies:
        copy.wait()
    d_act = sum_y[x] + ((in_x[0] + in_x[1]) + in_x[2])
    value = emb[x, y, z, core].astype(F32)
    sigmoid = 1.0 / (1.0 + jnp.exp(-value))
    d_emb = d_act * sigmoid * (1.0 + value * (1.0 - sigmoid))
    d_emb = jnp.concatenate([d_emb, jnp.zeros((HEAD - NCLIP, HEAD), F32)], axis=0).T
    result = lax.dot_general(
        d_emb[0:EMB, 0:NCLIP], sins[...], NN,
        precision=lax.Precision.HIGHEST, preferred_element_type=F32,
    )
    time_grad[...] = result

    sent = buf.at[:, :, pl.ds(0, CLIP - ROWS), :]
    pltpu.make_async_copy(sent, sent, in_send).wait()
    sent = ost.at[:, :, pl.ds(0, CLIP - ROWS), :]
    pltpu.make_async_copy(sent, sent, out_send).wait()
    for which, target in enumerate(targets):
        pltpu.make_async_copy(target, target, out_recv.at[which]).wait()


def per_device(query_rows, key_rows, value_rows, timestep, time_weight, gate_weight, cotangent):
    anywhere = pl.BlockSpec(memory_space=pl.ANY)
    vmem = pl.BlockSpec(memory_space=pltpu.VMEM)
    rows = jax.ShapeDtypeStruct((ROWS, DH), BF16)
    blocks = (SPAN, 2, 4, 2)
    outs = pl.pallas_call(
        kernel,
        out_shape=(
            rows, rows, rows, rows,
            jax.ShapeDtypeStruct((EMB, FREQ), F32),
            jax.ShapeDtypeStruct((COLS, D), F32),
        ),
        in_specs=[pl.BlockSpec(memory_space=pltpu.SMEM)] + [anywhere] * 4 + [vmem] * 2,
        out_specs=(anywhere,) * 4 + (vmem,) * 2,
        scratch_shapes=[
            pltpu.VMEM((OWN, 4, CLIP, HEAD), BF16),
            pltpu.VMEM((OWN, 4, CLIP, HEAD), BF16),
            pltpu.VMEM(blocks + (NCLIP, HEAD), BF16),
            pltpu.VMEM((NCLIP, HEAD), F32),
            pltpu.VMEM((NCLIP, D), BF16),
            pltpu.VMEM((NCLIP, FREQ), F32),
            pltpu.VMEM((COLS, HEAD), F32),
            pltpu.VMEM((COLS, HEAD), F32),
            pltpu.VMEM(blocks[1:] + (COLS, HEAD), F32),
            pltpu.VMEM((OWN, HEAD, HEAD), F32),
            pltpu.VMEM((8, HEAD), F32),
            pltpu.VMEM((2,) + blocks[1:] + (8, HEAD), F32),
            pltpu.VMEM(blocks + (NCLIP, HEAD), F32),
            pltpu.VMEM(blocks[:3] + (NCLIP, HEAD), F32),
            pltpu.VMEM(blocks[:2] + (NCLIP, HEAD), F32),
            pltpu.VMEM(blocks[:1] + (NCLIP, HEAD), F32),
            pltpu.VMEM(blocks[:3] + (NCLIP, HEAD), F32),
            pltpu.VMEM((3,) + blocks[:2] + (NCLIP, HEAD), F32),
            pltpu.VMEM(blocks[:1] + (NCLIP, HEAD), F32),
            pltpu.VMEM((3, NCLIP, HEAD), F32),
            pltpu.VMEM((HEAD, CLIP), BF16),
            pltpu.VMEM((HEAD, CLIP), BF16),
            pltpu.VMEM((CLIP, HEAD), F32),
            pltpu.VMEM((CLIP, HEAD), F32),
            pltpu.SemaphoreType.DMA((28,)),
            pltpu.SemaphoreType.DMA((28,)),
            pltpu.SemaphoreType.DMA,
            pltpu.SemaphoreType.DMA((OWN,)),
            pltpu.SemaphoreType.DMA,
            pltpu.SemaphoreType.DMA((4,)),
        ],
        compiler_params=pltpu.CompilerParams(
            collective_id=0, has_side_effects=True, vmem_limit_bytes=56 * 2**20
        ),
    )(
        timestep, query_rows, key_rows, value_rows, cotangent,
        time_weight[0].T, gate_weight[0].T,
    )
    gated, query_grad, key_grad, value_grad, time_grad, gate_grad = outs
    return gated, query_grad, key_grad, value_grad, time_grad.T[None], gate_grad.T[None]


def solution(mesh):
    return jax.shard_map(
        per_device,
        mesh=mesh,
        in_specs=(
            P(("expert", "fsdp"), None),
            P(("expert", "fsdp"), None),
            P(("expert", "fsdp"), None),
            P(),
            P("expert", None, "fsdp"),
            P("expert", None, "fsdp"),
            P(("expert", "fsdp"), None),
        ),
        out_specs=(
            P(("expert", "fsdp"), None),
            P(("expert", "fsdp"), None),
            P(("expert", "fsdp"), None),
            P(("expert", "fsdp"), None),
            P("expert", None, "fsdp"),
            P("expert", None, "fsdp"),
        ),
        check_vma=False,
    )
```

time: 1480 us -> 133 us (0.09); the launches traced: 1450 us -> 133 us
  waiting for transfers between devices: 920 us -> 0 us
  blocking collectives: 268 us -> 0 us
  local copies, waits for them, and re-layouts: 144 us -> 8.73 us
  Pallas kernels: 0 us -> 124 us
  matrix products: 65.7 us -> 0 us
  other arithmetic: 32.4 us -> 0 us
    unnamed x4 -> x0, waiting for transfers between devices: 920 us -> none
    all_gather x2 -> x0, blocking collectives: 258 us -> none  [the longest x1 178 us: per_device(): embedding = lax.all_gather(emb_cols, 'fsdp', axis=1, tiled=True)]
    pallas_call x0 -> x1, Pallas kernels: none -> 124 us  [per_device(): pl.pallas_call(kernel, out_shape=(rows, rows, rows, rows, jax.ShapeDtypeS...]
    dot_general x9 -> x0, matrix products: 49.8 us -> none  [the longest x1 14.8 us: per_device(): jnp.einsum('qhd,khd->hqk', d_heads, values_all, preferred_element_type=jn...]
    slice x2 -> x0, local copies, waits for them, and re-layouts: 47.9 us -> none  [the longest x1 38.5 us: per_device(): summed = partial_grads[0]]
    another operation x3 -> x0, local copies, waits for them, and re-layouts: 36.4 us -> none  [per_device(): jnp.stack([key_part.reshape(SPAN, row_count, -1), value_part.reshape(SPAN...]
    unnamed x58 -> x16, local copies, waits for them, and re-layouts: 42.3 us -> 8.73 us
  transfers between devices with their start and end apart: 9 -> 0, of which waited for: 2 -> 0; matrix products, arithmetic and copies ran while one was open for 3% -> 0% of each run, Pallas kernels for 0% -> 0%
where the time goes in v1:
time: 133 us
  Pallas kernels  124 us (93%)
  local copies, waits for them, and re-layouts  8.73 us (7%)
    pallas_call x1, Pallas kernels, per_device(): pl.pallas_call(kernel, out_shape=(rows, rows, rows, rows, jax.ShapeDtypeS...  124 us
    unnamed x16, local copies, waits for them, and re-layouts  8.73 us

profile of v1, /device:TPU:24, one launch (start us, length us, event | category | flops | bytes accessed | tf_op | source)
XLA Modules:
  0.0 133.1 jit_solution(14302892315250944148)
XLA Ops:
  0.6 123.7 %shard_map.118 = (bf16[256,2560]{1,0:T(8,128)(2,1)}, bf16[256,2560]{1,0:T(8,128)(2,1)}, bf16[256,2560]{1,0:T(8,128)(2,1)}, bf16[256,2560]{1,0:T(8,128)(2,1)}, f32[80,256]{1,0:T(8,128)}, /*index=5*/f32[40,5120]{1,0:T(8,128)}) custom-call(s32[32]{0:T(128)} %ts.1, bf16[256,2560]{1,0:T(8,128)(2,1)} %q_in.1, bf16[256,2560]{1,0:T(8,128)(2,1)} %k_in.1, ...), custom_call_target="tpu_custom_call" | custom-call | tf_op jit(solution)/shard_map/pallas_call | solution.py:319
  124.4 0.0 copy-start.2
  124.4 2.6 %copy.19 = bf16[256,2560]{1,0:T(8,128)(2,1)} copy(bf16[256,2560]{1,0:T(8,128)(2,1)} %get-tuple-element.24) | data formatting | bytes 2621440
  127.0 0.0 copy-done.2
  127.0 0.0 copy-start.1
  127.0 1.1 copy.20
  128.0 0.7 copy-done.1
  128.7 0.0 copy-start
  128.7 1.1 copy.21
  129.8 0.7 copy-done
  130.5 0.0 copy-start.4
  130.5 0.0 copy-start.3
  130.5 1.1 copy.22
  131.6 0.0 copy-done.4
  131.6 0.6 copy.23
  132.2 0.0 copy-done.3
  132.2 0.9 copy.24
Async XLA Ops:
  124.4 2.6 %copy-start.2 = (bf16[256,2560]{1,0:T(8,128)(2,1)S(1)}, bf16[256,2560]{1,0:T(8,128)(2,1)}, u32[]{:S(2)}) copy-start(bf16[256,2560]{1,0:T(8,128)(2,1)} %get-tuple-element.25) | copy-start | bytes 3932164
  127.0 1.8 %copy-start.1 = (bf16[256,2560]{1,0:T(8,128)(2,1)S(1)}, bf16[256,2560]{1,0:T(8,128)(2,1)}, u32[]{:S(2)}) copy-start(bf16[256,2560]{1,0:T(8,128)(2,1)} %get-tuple-element.26) | copy-start | bytes 3932164
  128.7 1.8 %copy-start = (bf16[256,2560]{1,0:T(8,128)(2,1)S(1)}, bf16[256,2560]{1,0:T(8,128)(2,1)}, u32[]{:S(2)}) copy-start(bf16[256,2560]{1,0:T(8,128)(2,1)} %get-tuple-element.27) | copy-start | bytes 3932164
  130.5 1.1 copy-start.4
  130.5 1.7 %copy-start.3 = (f32[40,5120]{1,0:T(8,128)S(1)}, f32[40,5120]{1,0:T(8,128)}, u32[]{:S(2)}) copy-start(f32[40,5120]{1,0:T(8,128)} %get-tuple-element.17) | copy-start | bytes 2457604

commit v2 on v1

--- a/solution.py
+++ b/solution.py
@@ -45,12 +45,12 @@
 
 
 def kernel(
-    ts, q_in, k_in, v_in, c_in, tw, gw,
+    ts_in, q_in, k_in, v_in, c_in, tw_in, gw_in,
     gated, query_grad, key_grad, value_grad, time_grad, gate_grad,
-    buf, ost, emb, own_emb, act, sins, cols, cols_in, table, gate_rows,
+    ts, tw, gw, buf, ost, emb, own_emb, act, sins, cols, cols_in, table, gate_rows,
     dg_own, dg_all, parts, sum_core, sum_z, sum_y, in_core, in_z, in_y, in_x,
     key_t, value_t, key_acc, value_acc,
-    send_sems, recv_sems, in_send, in_recv, out_send, out_recv,
+    ready, weight_sems, send_sems, recv_sems, in_send, in_recv, out_send, out_recv,
 ):
     half = lax.axis_index("expert")
     fsdp = lax.axis_index("fsdp")
@@ -70,11 +70,23 @@
     y_peer = place(x, 1 - y, z, core)
     core_peer = place(x, y, z, 1 - core)
     half_peer = {"expert": 1 - half}
-    peers = x_peers + z_peers + [y_peer, core_peer, half_peer]
 
     barrier = pltpu.get_barrier_semaphore()
-    for peer in peers:
+    ahead = [z < p for p in z_at] + [y == 0, core == 1, half == 0]
+    others = z_peers + [y_peer, core_peer, half_peer]
+    for peer in x_peers:
         pl.semaphore_signal(barrier, inc=1, device_id=peer, device_id_type=MESH)
+    for first, peer in zip(ahead, others):
+        @pl.when(first)
+        def _():
+            pl.semaphore_signal(barrier, inc=1, device_id=peer, device_id_type=MESH)
+
+    step_copy = pltpu.make_async_copy(ts_in, ts, weight_sems.at[2])
+    step_copy.start()
+    time_copy = pltpu.make_async_copy(tw_in, tw, weight_sems.at[0])
+    time_copy.start()
+    gate_copy = pltpu.make_async_copy(gw_in, gw, weight_sems.at[1])
+    gate_copy.start()
 
     used = [0]
 
@@ -99,10 +111,44 @@
         for copy in begin(moves):
             copy.wait()
 
+    pl.semaphore_wait(barrier, 3 + z + y + (1 - core) + half)
+    for first, peer in zip(ahead, others):
+        @pl.when(jnp.logical_not(first))
+        def _():
+            pl.semaphore_signal(ready, inc=1, device_id=peer, device_id_type=MESH)
+
+    sources = (q_in, k_in, v_in, c_in)
+
+    def send_part(head, which):
+        source = sources[which]
+        target = buf.at[head, which, pl.ds(pl.multiple_of(x * ROWS, ROWS), ROWS), :]
+        for to, peer in zip(x_at, x_peers):
+            pltpu.make_async_remote_copy(
+                src_ref=source.at[:, pl.ds(pl.multiple_of((to * OWN + head) * HEAD, HEAD), HEAD)],
+                dst_ref=target,
+                send_sem=in_send,
+                recv_sem=in_recv.at[head],
+                device_id=peer,
+                device_id_type=MESH,
+            ).start()
+        pltpu.make_async_copy(
+            source.at[:, pl.ds(pl.multiple_of((x * OWN + head) * HEAD, HEAD), HEAD)],
+            target,
+            in_recv.at[head],
+        ).start()
+
+    def send_head(head, carry):
+        for which in range(4):
+            send_part(head, which)
+        return carry
+
+    send_part(0, 0)
+
     row = lax.broadcasted_iota(jnp.int32, (NCLIP, HEAD), 0)
     lane = lax.broadcasted_iota(jnp.int32, (8, HEAD), 1)
     step_rows = jnp.zeros((NCLIP, HEAD), jnp.int32)
     step_lanes = jnp.zeros((8, HEAD), jnp.int32)
+    step_copy.wait()
     for clip in range(NCLIP):
         step_rows = jnp.where(row == clip, ts[clip], step_rows)
         step_lanes = jnp.where(lane == clip, ts[clip], step_lanes)
@@ -114,38 +160,24 @@
     angles = step_rows.astype(F32) * frequency
     sins[:, 0:HEAD] = jnp.cos(angles)
     sins[:, HEAD:FREQ] = jnp.sin(angles)
+    time_copy.wait()
     emb_cols = exact_dot(sins[...], tw[...], NT)
     own_emb[...] = jnp.zeros(own_emb.shape, F32)
     own_emb[:, 0:EMB] = emb_cols
     emb[x, y, z, core] = own_emb[...].astype(BF16)
-
-    pl.semaphore_wait(barrier, len(peers))
-
     first = begin([(emb.at[x, y, z, core], emb.at[x, y, z, core], peer) for peer in x_peers])
-    sources = (q_in, k_in, v_in, c_in)
-
-    def send_head(head, carry):
-        for which, source in enumerate(sources):
-            for to, peer in zip(x_at, x_peers):
-                pltpu.make_async_remote_copy(
-                    src_ref=source.at[:, pl.ds(pl.multiple_of((to * OWN + head) * HEAD, HEAD), HEAD)],
-                    dst_ref=buf.at[head, which, pl.ds(pl.multiple_of(x * ROWS, ROWS), ROWS), :],
-                    send_sem=in_send,
-                    recv_sem=in_recv.at[head],
-                    device_id=peer,
-                    device_id_type=MESH,
-                ).start()
-            pltpu.make_async_copy(
-                source.at[:, pl.ds(pl.multiple_of((x * OWN + head) * HEAD, HEAD), HEAD)],
-                buf.at[head, which, pl.ds(pl.multiple_of(x * ROWS, ROWS), ROWS), :],
-                in_recv.at[head],
-            ).start()
-        return carry
-
-    lax.fori_loop(0, OWN, send_head, 0)
+    for which in range(1, 4):
+        send_part(0, which)
+    lax.fori_loop(1, OWN, send_head, 0)
 
     for copy in first:
         copy.wait()
+    later = (3 - z) + (1 - y) + core + (1 - half)
+
+    @pl.when(later > 0)
+    def _():
+        pl.semaphore_wait(ready, later)
+
     exchange([(emb.at[:, y, z, core], emb.at[:, y, z, core], y_peer)])
     exchange([(emb.at[:, :, z, core], emb.at[:, :, z, core], peer) for peer in z_peers])
     exchange([(emb.at[:, :, :, core], emb.at[:, :, :, core], core_peer)])
@@ -159,6 +191,7 @@
         return carry
 
     lax.fori_loop(0, 8, activate, 0)
+    gate_copy.wait()
     gate_cols = dot(gw[...], act[...], NT).astype(BF16).astype(F32)
     cols[...] = jnp.zeros(cols.shape, F32)
     cols[:, 0:NCLIP] = gate_cols
@@ -311,21 +344,32 @@
         pltpu.make_async_copy(target, target, out_recv.at[which]).wait()
 
 
+def deliver(*refs):
+    count = len(refs) // 2
+    sems = refs[-1]
+    copies = [
+        pltpu.make_async_copy(refs[i], refs[count + i], sems.at[i]) for i in range(count)
+    ]
+    for copy in copies:
+        copy.start()
+    for copy in copies:
+        copy.wait()
+
+
 def per_device(query_rows, key_rows, value_rows, timestep, time_weight, gate_weight, cotangent):
-    anywhere = pl.BlockSpec(memory_space=pl.ANY)
+    hbm = pl.BlockSpec(memory_space=pltpu.HBM)
     vmem = pl.BlockSpec(memory_space=pltpu.VMEM)
-    rows = jax.ShapeDtypeStruct((ROWS, DH), BF16)
     blocks = (SPAN, 2, 4, 2)
+    shapes = [((ROWS, DH), BF16)] * 4 + [((EMB, FREQ), F32), ((COLS, D), F32)]
     outs = pl.pallas_call(
         kernel,
-        out_shape=(
-            rows, rows, rows, rows,
-            jax.ShapeDtypeStruct((EMB, FREQ), F32),
-            jax.ShapeDtypeStruct((COLS, D), F32),
-        ),
-        in_specs=[pl.BlockSpec(memory_space=pltpu.SMEM)] + [anywhere] * 4 + [vmem] * 2,
-        out_specs=(anywhere,) * 4 + (vmem,) * 2,
+        out_shape=tuple(pltpu.VMEM(shape, dtype) for shape, dtype in shapes),
+        in_specs=[hbm] * 7,
+        out_specs=(vmem,) * 6,
         scratch_shapes=[
+            pltpu.SMEM((NCLIP,), jnp.int32),
+            pltpu.VMEM((EMB, FREQ), BF16),
+            pltpu.VMEM((COLS, D), BF16),
             pltpu.VMEM((OWN, 4, CLIP, HEAD), BF16),
             pltpu.VMEM((OWN, 4, CLIP, HEAD), BF16),
             pltpu.VMEM(blocks + (NCLIP, HEAD), BF16),
@@ -350,6 +394,8 @@
             pltpu.VMEM((HEAD, CLIP), BF16),
             pltpu.VMEM((CLIP, HEAD), F32),
             pltpu.VMEM((CLIP, HEAD), F32),
+            pltpu.SemaphoreType.REGULAR,
+            pltpu.SemaphoreType.DMA((3,)),
             pltpu.SemaphoreType.DMA((28,)),
             pltpu.SemaphoreType.DMA((28,)),
             pltpu.SemaphoreType.DMA,
@@ -358,12 +404,26 @@
             pltpu.SemaphoreType.DMA((4,)),
         ],
         compiler_params=pltpu.CompilerParams(
-            collective_id=0, has_side_effects=True, vmem_limit_bytes=56 * 2**20
+            collective_id=0, has_side_effects=True, vmem_limit_bytes=40 * 2**20
         ),
     )(
-        timestep, query_rows, key_rows, value_rows, cotangent,
-        time_weight[0].T, gate_weight[0].T,
+        *[
+            pltpu.with_memory_space_constraint(array, pltpu.HBM)
+            for array in (
+                timestep, query_rows, key_rows, value_rows, cotangent,
+                time_weight[0].T, gate_weight[0].T,
+            )
+        ],
     )
+    outs = [pltpu.with_memory_space_constraint(out, pltpu.VMEM) for out in outs]
+    outs = pl.pallas_call(
+        deliver,
+        out_shape=tuple(jax.ShapeDtypeStruct(shape, dtype) for shape, dtype in shapes),
+        in_specs=[vmem] * 6,
+        out_specs=(hbm,) * 6,
+        scratch_shapes=[pltpu.SemaphoreType.DMA((6,))],
+        compiler_params=pltpu.CompilerParams(vmem_limit_bytes=4 * 2**20),
+    )(*outs)
     gated, query_grad, key_grad, value_grad, time_grad, gate_grad = outs
     return gated, query_grad, key_grad, value_grad, time_grad.T[None], gate_grad.T[None]
 

time: 133 us -> 123 us (0.925)
  local copies, waits for them, and re-layouts: 8.73 us -> 0 us
  Pallas kernels: 124 us -> 122 us
    unnamed x16 -> x0, local copies, waits for them, and re-layouts: 8.73 us -> none
    pallas_call x1 -> x2, Pallas kernels: 124 us -> 122 us  [the longest x1 119 us: per_device(): pl.pallas_call(kernel, out_shape=tuple((pltpu.VMEM(shape, dtype) for shap...]
where the time goes in v2:
time: 123 us; the launch traced here: 122 us
  Pallas kernels  122 us (99%)
    pallas_call x1, Pallas kernels, per_device(): pl.pallas_call(kernel, out_shape=tuple((pltpu.VMEM(shape, dtype) for shap...  119 us
    pallas_call x1, Pallas kernels, per_device(): pl.pallas_call(deliver, out_shape=tuple((jax.ShapeDtypeStruct(shape, dtyp...  2.7 us

profile of v2, /device:TPU:24, one launch (start us, length us, event | category | flops | bytes accessed | tf_op | source)
XLA Modules:
  0.0 122.4 jit_solution(5560241519282357262)
XLA Ops:
  0.6 119.1 %shard_map.118 = (bf16[256,2560]{1,0:T(8,128)(2,1)S(1)}, bf16[256,2560]{1,0:T(8,128)(2,1)S(1)}, bf16[256,2560]{1,0:T(8,128)(2,1)S(1)}, bf16[256,2560]{1,0:T(8,12...) custom-call(s32[32]{0:T(128)} %ts_in.1, bf16[256,2560]{1,0:T(8,128)(2,1)} %q_in.1, bf16[256,2560]{1,0:T(8,128)(2,1)} %k_in.1, ...), custom_call_target="tpu_custom_call" | custom-call | tf_op jit(solution)/shard_map/pallas_call | solution.py:364
  119.8 2.7 %shard_map.119 = (bf16[256,2560]{1,0:T(8,128)(2,1)}, bf16[256,2560]{1,0:T(8,128)(2,1)}, bf16[256,2560]{1,0:T(8,128)(2,1)}, bf16[256,2560]{1,0:T(8,128)(2,1)}, f32[80,256]{1,0:T(8,128)}, /*index=5*/f32[40,5120]{1,0:T(8,128)}) custom-call(bf16[256,2560]{1,0:T(8,128)(2,1)S(1)} %get-tuple-element.18.refs_0_, bf16[256,2560]{1,0:T(8,128)(2,1)S(1)} %get-tuple-element.19.refs_1_, ...), custom_call_target="tpu_custom_call" | custom-call | tf_op jit(solution)/shard_map/pallas_call | solution.py:419

commit v3 on v2

--- a/solution.py
+++ b/solution.py
@@ -15,6 +15,7 @@
 OWN = 5
 CLIP = SPAN * ROWS
 NCLIP = 32
+NOWN = 16
 EMB = 80
 COLS = 40
 D = 5120
@@ -48,7 +49,7 @@
     ts_in, q_in, k_in, v_in, c_in, tw_in, gw_in,
     gated, query_grad, key_grad, value_grad, time_grad, gate_grad,
     ts, tw, gw, buf, ost, emb, own_emb, act, sins, cols, cols_in, table, gate_rows,
-    dg_own, dg_all, parts, sum_core, sum_z, sum_y, in_core, in_z, in_y, in_x,
+    dg_own, dg_all, parts, sum_core, sum_z, sum_y, in_core, in_z, in_y, in_x, half_sums, pick_clip,
     key_t, value_t, key_acc, value_acc,
     ready, weight_sems, send_sems, recv_sems, in_send, in_recv, out_send, out_recv,
 ):
@@ -112,11 +113,6 @@
             copy.wait()
 
     pl.semaphore_wait(barrier, 3 + z + y + (1 - core) + half)
-    for first, peer in zip(ahead, others):
-        @pl.when(jnp.logical_not(first))
-        def _():
-            pl.semaphore_signal(ready, inc=1, device_id=peer, device_id_type=MESH)
-
     sources = (q_in, k_in, v_in, c_in)
 
     def send_part(head, which):
@@ -143,21 +139,27 @@
         return carry
 
     send_part(0, 0)
-
-    row = lax.broadcasted_iota(jnp.int32, (NCLIP, HEAD), 0)
-    lane = lax.broadcasted_iota(jnp.int32, (8, HEAD), 1)
-    step_rows = jnp.zeros((NCLIP, HEAD), jnp.int32)
-    step_lanes = jnp.zeros((8, HEAD), jnp.int32)
+    for first, peer in zip(ahead, others):
+        @pl.when(jnp.logical_not(first))
+        def _():
+            pl.semaphore_signal(ready, inc=1, device_id=peer, device_id_type=MESH)
+
+    row = lax.broadcasted_iota(jnp.int32, (NOWN, HEAD), 0)
+    lane = lax.broadcasted_iota(jnp.int32, (NOWN, HEAD), 1)
+    steps = jnp.zeros((NOWN, HEAD), jnp.int32)
+    chosen = jnp.zeros((NOWN, HEAD), F32)
+    rank = jnp.int32(0)
     step_copy.wait()
     for clip in range(NCLIP):
-        step_rows = jnp.where(row == clip, ts[clip], step_rows)
-        step_lanes = jnp.where(lane == clip, ts[clip], step_lanes)
-    own_rows = (step_rows >= BOUNDARY).astype(jnp.int32) == half
-    own_lanes = (step_lanes >= BOUNDARY).astype(jnp.int32) == half
-
-    index = lax.broadcasted_iota(jnp.int32, (NCLIP, HEAD), 1).astype(F32)
-    frequency = jnp.exp(-math.log(10000.0) * index / (FREQ // 2))
-    angles = step_rows.astype(F32) * frequency
+        own = (ts[clip] >= BOUNDARY).astype(jnp.int32) == half
+        hit = row == jnp.where(own, rank, -1)
+        steps = jnp.where(hit, ts[clip], steps)
+        chosen = jnp.where(hit & (lane == clip), 1.0, chosen)
+        rank = rank + jnp.where(own, 1, 0)
+    pick_clip[...] = chosen.astype(BF16)
+
+    frequency = jnp.exp(-math.log(10000.0) * lane.astype(F32) / (FREQ // 2))
+    angles = steps.astype(F32) * frequency
     sins[:, 0:HEAD] = jnp.cos(angles)
     sins[:, HEAD:FREQ] = jnp.sin(angles)
     time_copy.wait()
@@ -165,6 +167,7 @@
     own_emb[...] = jnp.zeros(own_emb.shape, F32)
     own_emb[:, 0:EMB] = emb_cols
     emb[x, y, z, core] = own_emb[...].astype(BF16)
+
     first = begin([(emb.at[x, y, z, core], emb.at[x, y, z, core], peer) for peer in x_peers])
     for which in range(1, 4):
         send_part(0, which)
@@ -192,11 +195,10 @@
 
     lax.fori_loop(0, 8, activate, 0)
     gate_copy.wait()
-    gate_cols = dot(gw[...], act[...], NT).astype(BF16).astype(F32)
-    cols[...] = jnp.zeros(cols.shape, F32)
-    cols[:, 0:NCLIP] = gate_cols
+    gate_cols = dot(gw[...], act[...], NT).astype(BF16)
+    cols[...] = dot(gate_cols, pick_clip[...])
     exchange([(cols, cols_in, half_peer)])
-    table[y, z, core] = jnp.where(own_lanes[0:1], cols[...], cols_in[...])
+    table[y, z, core] = cols[...] + cols_in[...]
     exchange([(table.at[y, z, core], table.at[y, z, core], peer) for peer in z_peers])
     exchange([(table.at[y, :, core], table.at[y, :, core], y_peer)])
     exchange([(table.at[:, :, core], table.at[:, :, core], core_peer)])
@@ -278,17 +280,16 @@
     exchange([(dg_all.at[half, :, :, core], dg_all.at[half, :, :, core], core_peer)])
     exchange([(dg_all.at[half], dg_all.at[half], half_peer)])
     everything = dg_all[...].reshape(NCLIP, 8, HEAD)
-    d_rows = jnp.zeros((NCLIP, COLS), F32)
-    d_cols = jnp.zeros((COLS, NCLIP), F32)
+    d_rows = jnp.zeros((NOWN, COLS), F32)
+    d_cols = jnp.zeros((COLS, NOWN), F32)
     pick_row = lax.broadcasted_iota(jnp.int32, (COLS, HEAD), 0) + plane * COLS
     pick_lane = lax.broadcasted_iota(jnp.int32, (COLS, HEAD), 1)
     for head in range(OWN):
         pick = (pick_row == pick_lane + head * HEAD).astype(F32).astype(BF16)
         for part in split3(everything[:, head, :]):
+            part = dot(pick_clip[:, 0:NCLIP], part).astype(BF16)
             d_rows = d_rows + dot(part, pick, NT)
             d_cols = d_cols + dot(pick, part, NT)
-    d_rows = jnp.where(own_rows[:, 0:COLS], d_rows, 0.0)
-    d_cols = jnp.where(own_lanes[0:1, 0:NCLIP], d_cols, 0.0)
     row_parts = split3(d_rows)
     col_parts = split3(d_cols)
     parts[...] = jnp.zeros(parts.shape, F32)
@@ -321,17 +322,18 @@
     sum_z[...] = sum_core[:, :, z] + ((in_z[0] + in_z[1]) + in_z[2])
     exchange([(sum_z.at[:, 1 - y], in_y, y_peer)])
     sum_y[...] = sum_z[:, y] + in_y[...]
-    copies = begin([(sum_y.at[p], in_x.at[d], peer) for d, (p, peer) in enumerate(zip(x_at, x_peers))])
+    half_sums[...] = sum_y[...].astype(BF16)
+    copies = begin([(half_sums.at[p], in_x.at[d], peer) for d, (p, peer) in enumerate(zip(x_at, x_peers))])
     send_out(OWN - 1)
     for copy in copies:
         copy.wait()
-    d_act = sum_y[x] + ((in_x[0] + in_x[1]) + in_x[2])
+    d_act = sum_y[x] + ((in_x[0].astype(F32) + in_x[1].astype(F32)) + in_x[2].astype(F32))
     value = emb[x, y, z, core].astype(F32)
     sigmoid = 1.0 / (1.0 + jnp.exp(-value))
     d_emb = d_act * sigmoid * (1.0 + value * (1.0 - sigmoid))
-    d_emb = jnp.concatenate([d_emb, jnp.zeros((HEAD - NCLIP, HEAD), F32)], axis=0).T
+    d_emb = jnp.concatenate([d_emb, jnp.zeros((HEAD - NOWN, HEAD), F32)], axis=0).T
     result = lax.dot_general(
-        d_emb[0:EMB, 0:NCLIP], sins[...], NN,
+        d_emb[0:EMB, 0:NOWN], sins[...], NN,
         precision=lax.Precision.HIGHEST, preferred_element_type=F32,
     )
     time_grad[...] = result
@@ -372,24 +374,26 @@
             pltpu.VMEM((COLS, D), BF16),
             pltpu.VMEM((OWN, 4, CLIP, HEAD), BF16),
             pltpu.VMEM((OWN, 4, CLIP, HEAD), BF16),
-            pltpu.VMEM(blocks + (NCLIP, HEAD), BF16),
-            pltpu.VMEM((NCLIP, HEAD), F32),
-            pltpu.VMEM((NCLIP, D), BF16),
-            pltpu.VMEM((NCLIP, FREQ), F32),
+            pltpu.VMEM(blocks + (NOWN, HEAD), BF16),
+            pltpu.VMEM((NOWN, HEAD), F32),
+            pltpu.VMEM((NOWN, D), BF16),
+            pltpu.VMEM((NOWN, FREQ), F32),
             pltpu.VMEM((COLS, HEAD), F32),
             pltpu.VMEM((COLS, HEAD), F32),
             pltpu.VMEM(blocks[1:] + (COLS, HEAD), F32),
             pltpu.VMEM((OWN, HEAD, HEAD), F32),
             pltpu.VMEM((8, HEAD), F32),
             pltpu.VMEM((2,) + blocks[1:] + (8, HEAD), F32),
-            pltpu.VMEM(blocks + (NCLIP, HEAD), F32),
-            pltpu.VMEM(blocks[:3] + (NCLIP, HEAD), F32),
-            pltpu.VMEM(blocks[:2] + (NCLIP, HEAD), F32),
-            pltpu.VMEM(blocks[:1] + (NCLIP, HEAD), F32),
-            pltpu.VMEM(blocks[:3] + (NCLIP, HEAD), F32),
-            pltpu.VMEM((3,) + blocks[:2] + (NCLIP, HEAD), F32),
-            pltpu.VMEM(blocks[:1] + (NCLIP, HEAD), F32),
-            pltpu.VMEM((3, NCLIP, HEAD), F32),
+            pltpu.VMEM(blocks + (NOWN, HEAD), F32),
+            pltpu.VMEM(blocks[:3] + (NOWN, HEAD), F32),
+            pltpu.VMEM(blocks[:2] + (NOWN, HEAD), F32),
+            pltpu.VMEM(blocks[:1] + (NOWN, HEAD), F32),
+            pltpu.VMEM(blocks[:3] + (NOWN, HEAD), F32),
+            pltpu.VMEM((3,) + blocks[:2] + (NOWN, HEAD), F32),
+            pltpu.VMEM(blocks[:1] + (NOWN, HEAD), F32),
+            pltpu.VMEM((3, NOWN, HEAD), BF16),
+            pltpu.VMEM((SPAN, NOWN, HEAD), BF16),
+            pltpu.VMEM((NOWN, HEAD), BF16),
             pltpu.VMEM((HEAD, CLIP), BF16),
             pltpu.VMEM((HEAD, CLIP), BF16),
             pltpu.VMEM((CLIP, HEAD), F32),

time: 123 us -> 122 us (level)
  no operation moved by 1% of the time
where the time goes in v3:
time: 122 us
  Pallas kernels  121 us (99%)
    pallas_call x1, Pallas kernels, per_device(): pl.pallas_call(kernel, out_shape=tuple((pltpu.VMEM(shape, dtype) for shap...  118 us
    pallas_call x1, Pallas kernels, per_device(): pl.pallas_call(deliver, out_shape=tuple((jax.ShapeDtypeStruct(shape, dtyp...  2.7 us

profile of v3, /device:TPU:24, one launch (start us, length us, event | category | flops | bytes accessed | tf_op | source)
XLA Modules:
  0.0 121.7 jit_solution(15570374447476882286)
XLA Ops:
  0.6 118.4 %shard_map.118 = (bf16[256,2560]{1,0:T(8,128)(2,1)S(1)}, bf16[256,2560]{1,0:T(8,128)(2,1)S(1)}, bf16[256,2560]{1,0:T(8,128)(2,1)S(1)}, bf16[256,2560]{1,0:T(8,12...) custom-call(s32[32]{0:T(128)} %ts_in.1, bf16[256,2560]{1,0:T(8,128)(2,1)} %q_in.1, bf16[256,2560]{1,0:T(8,128)(2,1)} %k_in.1, ...), custom_call_target="tpu_custom_call" | custom-call | tf_op jit(solution)/shard_map/pallas_call | solution.py:366
  119.0 2.7 %shard_map.119 = (bf16[256,2560]{1,0:T(8,128)(2,1)}, bf16[256,2560]{1,0:T(8,128)(2,1)}, bf16[256,2560]{1,0:T(8,128)(2,1)}, bf16[256,2560]{1,0:T(8,128)(2,1)}, f32[80,256]{1,0:T(8,128)}, /*index=5*/f32[40,5120]{1,0:T(8,128)}) custom-call(bf16[256,2560]{1,0:T(8,128)(2,1)S(1)} %get-tuple-element.18.refs_0_, bf16[256,2560]{1,0:T(8,128)(2,1)S(1)} %get-tuple-element.19.refs_1_, ...), custom_call_target="tpu_custom_call" | custom-call | tf_op jit(solution)/shard_map/pallas_call | solution.py:423

commit v4 on v3

--- a/solution.py
+++ b/solution.py
@@ -84,8 +84,14 @@
 
     step_copy = pltpu.make_async_copy(ts_in, ts, weight_sems.at[2])
     step_copy.start()
-    time_copy = pltpu.make_async_copy(tw_in, tw, weight_sems.at[0])
-    time_copy.start()
+    time_copies = [
+        pltpu.make_async_copy(
+            tw_in.at[:, i * HEAD : (i + 1) * HEAD], tw.at[:, i * HEAD : (i + 1) * HEAD], weight_sems.at[3 * i]
+        )
+        for i in range(FREQ // HEAD)
+    ]
+    for copy in time_copies:
+        copy.start()
     gate_copy = pltpu.make_async_copy(gw_in, gw, weight_sems.at[1])
     gate_copy.start()
 
@@ -162,7 +168,8 @@
     angles = steps.astype(F32) * frequency
     sins[:, 0:HEAD] = jnp.cos(angles)
     sins[:, HEAD:FREQ] = jnp.sin(angles)
-    time_copy.wait()
+    for copy in time_copies:
+        copy.wait()
     emb_cols = exact_dot(sins[...], tw[...], NT)
     own_emb[...] = jnp.zeros(own_emb.shape, F32)
     own_emb[:, 0:EMB] = emb_cols
@@ -399,7 +406,7 @@
             pltpu.VMEM((CLIP, HEAD), F32),
             pltpu.VMEM((CLIP, HEAD), F32),
             pltpu.SemaphoreType.REGULAR,
-            pltpu.SemaphoreType.DMA((3,)),
+            pltpu.SemaphoreType.DMA((4,)),
             pltpu.SemaphoreType.DMA((28,)),
             pltpu.SemaphoreType.DMA((28,)),
             pltpu.SemaphoreType.DMA,

time: 122 us -> 122 us (level)
  no operation moved by 1% of the time
where the time goes in v4:
time: 122 us
  Pallas kernels  121 us (99%)
    pallas_call x1, Pallas kernels, per_device(): pl.pallas_call(kernel, out_shape=tuple((pltpu.VMEM(shape, dtype) for shap...  118 us
    pallas_call x1, Pallas kernels, per_device(): pl.pallas_call(deliver, out_shape=tuple((jax.ShapeDtypeStruct(shape, dtyp...  2.7 us

profile of v4, /device:TPU:24, one launch (start us, length us, event | category | flops | bytes accessed | tf_op | source)
XLA Modules:
  0.0 121.8 jit_solution(7723831971011985100)
XLA Ops:
  0.6 118.4 %shard_map.118 = (bf16[256,2560]{1,0:T(8,128)(2,1)S(1)}, bf16[256,2560]{1,0:T(8,128)(2,1)S(1)}, bf16[256,2560]{1,0:T(8,128)(2,1)S(1)}, bf16[256,2560]{1,0:T(8,12...) custom-call(s32[32]{0:T(128)} %ts_in.1, bf16[256,2560]{1,0:T(8,128)(2,1)} %q_in.1, bf16[256,2560]{1,0:T(8,128)(2,1)} %k_in.1, ...), custom_call_target="tpu_custom_call" | custom-call | tf_op jit(solution)/shard_map/pallas_call | solution.py:373
  119.1 2.7 %shard_map.119 = (bf16[256,2560]{1,0:T(8,128)(2,1)}, bf16[256,2560]{1,0:T(8,128)(2,1)}, bf16[256,2560]{1,0:T(8,128)(2,1)}, bf16[256,2560]{1,0:T(8,128)(2,1)}, f32[80,256]{1,0:T(8,128)}, /*index=5*/f32[40,5120]{1,0:T(8,128)}) custom-call(bf16[256,2560]{1,0:T(8,128)(2,1)S(1)} %get-tuple-element.18.refs_0_, bf16[256,2560]{1,0:T(8,128)(2,1)S(1)} %get-tuple-element.19.refs_1_, ...), custom_call_target="tpu_custom_call" | custom-call | tf_op jit(solution)/shard_map/pallas_call | solution.py:430

commit v5 on v3

--- a/solution.py
+++ b/solution.py
@@ -82,13 +82,6 @@
         def _():
             pl.semaphore_signal(barrier, inc=1, device_id=peer, device_id_type=MESH)
 
-    step_copy = pltpu.make_async_copy(ts_in, ts, weight_sems.at[2])
-    step_copy.start()
-    time_copy = pltpu.make_async_copy(tw_in, tw, weight_sems.at[0])
-    time_copy.start()
-    gate_copy = pltpu.make_async_copy(gw_in, gw, weight_sems.at[1])
-    gate_copy.start()
-
     used = [0]
 
     def begin(moves):
@@ -139,6 +132,18 @@
         return carry
 
     send_part(0, 0)
+    step_copy = pltpu.make_async_copy(ts_in, ts, weight_sems.at[2])
+    step_copy.start()
+    time_copies = [
+        pltpu.make_async_copy(
+            tw_in.at[:, i * HEAD : (i + 1) * HEAD], tw.at[:, i * HEAD : (i + 1) * HEAD], weight_sems.at[3 * i]
+        )
+        for i in range(FREQ // HEAD)
+    ]
+    for copy in time_copies:
+        copy.start()
+    gate_copy = pltpu.make_async_copy(gw_in, gw, weight_sems.at[1])
+    gate_copy.start()
     for first, peer in zip(ahead, others):
         @pl.when(jnp.logical_not(first))
         def _():
@@ -162,7 +167,8 @@
     angles = steps.astype(F32) * frequency
     sins[:, 0:HEAD] = jnp.cos(angles)
     sins[:, HEAD:FREQ] = jnp.sin(angles)
-    time_copy.wait()
+    for copy in time_copies:
+        copy.wait()
     emb_cols = exact_dot(sins[...], tw[...], NT)
     own_emb[...] = jnp.zeros(own_emb.shape, F32)
     own_emb[:, 0:EMB] = emb_cols
@@ -399,7 +405,7 @@
             pltpu.VMEM((CLIP, HEAD), F32),
             pltpu.VMEM((CLIP, HEAD), F32),
             pltpu.SemaphoreType.REGULAR,
-            pltpu.SemaphoreType.DMA((3,)),
+            pltpu.SemaphoreType.DMA((4,)),
             pltpu.SemaphoreType.DMA((28,)),
             pltpu.SemaphoreType.DMA((28,)),
             pltpu.SemaphoreType.DMA,

time: 122 us -> 122 us (level)
  no operation moved by 1% of the time
where the time goes in v5:
time: 122 us
  Pallas kernels  121 us (99%)
    pallas_call x1, Pallas kernels, per_device(): pl.pallas_call(kernel, out_shape=tuple((pltpu.VMEM(shape, dtype) for shap...  118 us
    pallas_call x1, Pallas kernels, per_device(): pl.pallas_call(deliver, out_shape=tuple((jax.ShapeDtypeStruct(shape, dtyp...  2.7 us

profile of v5, /device:TPU:24, one launch (start us, length us, event | category | flops | bytes accessed | tf_op | source)
XLA Modules:
  0.0 121.8 jit_solution(12428113137990054246)
XLA Ops:
  0.6 118.4 %shard_map.118 = (bf16[256,2560]{1,0:T(8,128)(2,1)S(1)}, bf16[256,2560]{1,0:T(8,128)(2,1)S(1)}, bf16[256,2560]{1,0:T(8,128)(2,1)S(1)}, bf16[256,2560]{1,0:T(8,12...) custom-call(s32[32]{0:T(128)} %ts_in.1, bf16[256,2560]{1,0:T(8,128)(2,1)} %q_in.1, bf16[256,2560]{1,0:T(8,128)(2,1)} %k_in.1, ...), custom_call_target="tpu_custom_call" | custom-call | tf_op jit(solution)/shard_map/pallas_call | solution.py:372
  119.1 2.7 %shard_map.119 = (bf16[256,2560]{1,0:T(8,128)(2,1)}, bf16[256,2560]{1,0:T(8,128)(2,1)}, bf16[256,2560]{1,0:T(8,128)(2,1)}, bf16[256,2560]{1,0:T(8,128)(2,1)}, f32[80,256]{1,0:T(8,128)}, /*index=5*/f32[40,5120]{1,0:T(8,128)}) custom-call(bf16[256,2560]{1,0:T(8,128)(2,1)S(1)} %get-tuple-element.18.refs_0_, bf16[256,2560]{1,0:T(8,128)(2,1)S(1)} %get-tuple-element.19.refs_1_, ...), custom_call_target="tpu_custom_call" | custom-call | tf_op jit(solution)/shard_map/pallas_call | solution.py:429

commit v6 on v4

--- a/solution.py
+++ b/solution.py
@@ -255,9 +255,10 @@
 
     targets = (gated, query_grad, key_grad, value_grad)
 
-    def send_out(head):
+    def send_out(head, arrays=range(4)):
         at = pl.ds(pl.multiple_of((x * OWN + head) * HEAD, HEAD), HEAD)
-        for which, target in enumerate(targets):
+        for which in arrays:
+            target = targets[which]
             for to, peer in zip(x_at, x_peers):
                 pltpu.make_async_remote_copy(
                     src_ref=ost.at[head, which, pl.ds(pl.multiple_of(to * ROWS, ROWS), ROWS), :],
@@ -280,6 +281,7 @@
 
     lax.fori_loop(0, OWN - 1, run_head, 0)
     attend(OWN - 1)
+    send_out(OWN - 1, (0, 1))
 
     dg_all[half, y, z, core] = dg_own[...]
     exchange([(dg_all.at[half, y, z, core], dg_all.at[half, y, z, core], peer) for peer in z_peers])
@@ -331,7 +333,7 @@
     sum_y[...] = sum_z[:, y] + in_y[...]
     half_sums[...] = sum_y[...].astype(BF16)
     copies = begin([(half_sums.at[p], in_x.at[d], peer) for d, (p, peer) in enumerate(zip(x_at, x_peers))])
-    send_out(OWN - 1)
+    send_out(OWN - 1, (2, 3))
     for copy in copies:
         copy.wait()
     d_act = sum_y[x] + ((in_x[0].astype(F32) + in_x[1].astype(F32)) + in_x[2].astype(F32))

time: 122 us -> 122 us (level)
  no operation moved by 1% of the time
where the time goes in v6:
time: 122 us
  Pallas kernels  121 us (99%)
    pallas_call x1, Pallas kernels, per_device(): pl.pallas_call(kernel, out_shape=tuple((pltpu.VMEM(shape, dtype) for shap...  118 us
    pallas_call x1, Pallas kernels, per_device(): pl.pallas_call(deliver, out_shape=tuple((jax.ShapeDtypeStruct(shape, dtyp...  2.7 us

profile of v6, /device:TPU:24, one launch (start us, length us, event | category | flops | bytes accessed | tf_op | source)
XLA Modules:
  0.0 121.8 jit_solution(15339877914920502590)
XLA Ops:
  0.6 118.4 %shard_map.118 = (bf16[256,2560]{1,0:T(8,128)(2,1)S(1)}, bf16[256,2560]{1,0:T(8,128)(2,1)S(1)}, bf16[256,2560]{1,0:T(8,128)(2,1)S(1)}, bf16[256,2560]{1,0:T(8,12...) custom-call(s32[32]{0:T(128)} %ts_in.1, bf16[256,2560]{1,0:T(8,128)(2,1)} %q_in.1, bf16[256,2560]{1,0:T(8,128)(2,1)} %k_in.1, ...), custom_call_target="tpu_custom_call" | custom-call | tf_op jit(solution)/shard_map/pallas_call | solution.py:375
  119.1 2.7 %shard_map.119 = (bf16[256,2560]{1,0:T(8,128)(2,1)}, bf16[256,2560]{1,0:T(8,128)(2,1)}, bf16[256,2560]{1,0:T(8,128)(2,1)}, bf16[256,2560]{1,0:T(8,128)(2,1)}, f32[80,256]{1,0:T(8,128)}, /*index=5*/f32[40,5120]{1,0:T(8,128)}) custom-call(bf16[256,2560]{1,0:T(8,128)(2,1)S(1)} %get-tuple-element.18.refs_0_, bf16[256,2560]{1,0:T(8,128)(2,1)S(1)} %get-tuple-element.19.refs_1_, ...), custom_call_target="tpu_custom_call" | custom-call | tf_op jit(solution)/shard_map/pallas_call | solution.py:432
